TPU v7x, 32 devices: a whole 2x2x4 slice. The times are simulated.
32 devices in a mesh: groups: 2 (over y), bricks: 4 (over z), sub: 4 (over x, core).
Axes of the slice: x: 2, y: 2, z: 4, core: 2. Of those that a mesh axis runs over, the one named last changes fastest.
Arguments:
- features: bfloat16 [32768, 256], P(('groups', 'bricks', 'sub')), parts along dimension 0, may hold values from -6 to 6
- active: int32 [64], P(('groups', 'bricks', 'sub')), parts along dimension 0, may hold values 0 or 1
- weight: bfloat16 [27, 256, 128], replicated, may hold values from -0.078125 to 0.078125
- cotangent: bfloat16 [32768, 128], P(('groups', 'bricks', 'sub')), parts along dimension 0, may hold values from -6 to 6
Outputs:
- conv_out: bfloat16 [32768, 128], P(('groups', 'bricks', 'sub')), parts along dimension 0
- grad_features: bfloat16 [32768, 256], P(('groups', 'bricks', 'sub')), parts along dimension 0
- grad_weight: bfloat16 [54, 256, 128], P('groups'), parts along dimension 0
There are 2 independent parts, one for each index of `groups`. A program takes and returns all parts, laid end to end along the dimension named above; an argument that names none is the same for every part. Nothing has to cross between parts.
All inputs are finite; a program needn't handle non-finite values. No bound on the sum of `active` on one device may be relied on, other than what follows from the above.
Results may differ from a plain program's by a relative error of at most 0.003.
Values may be sent and summed in bfloat16 or wider, within the bound.
A program may use at most 64 MiB of HBM per device.

v0:
```python
import math

import jax
import jax.numpy as jnp
from jax import lax
from jax.sharding import PartitionSpec as P

EDGE = 8


def from_behind(x, axis, by):
    devices = lax.axis_size(axis)
    pairs = [(i, i + by) for i in range(devices) if 0 <= i + by < devices]
    return lax.ppermute(x, axis, pairs)


def padded(x, sides, width):
    for axis, dim in sides:
        devices, length = (lax.axis_size(axis), x.shape[dim])
        up = [(i, (i + 1) % devices) for i in range(devices - 1)]
        down = [(j, i) for i, j in up]
        last = lax.slice_in_dim(x, length - width, length, axis=dim)
        leading = lax.slice_in_dim(x, 0, width, axis=dim)
        before = lax.ppermute(last, axis, up)
        after = lax.ppermute(leading, axis, down)
        x = jnp.concatenate([before, x, after], axis=dim)
    return x


def to_block(rows, bricks_dev):
    width = rows.shape[1]
    cube = rows.reshape(bricks_dev, EDGE, EDGE, EDGE, width)
    return cube.transpose(1, 2, 0, 3, 4).reshape(EDGE, EDGE, bricks_dev * EDGE, width)


def to_rows(block, bricks_dev):
    width = block.shape[3]
    cube = block.reshape(EDGE, EDGE, bricks_dev, EDGE, width)
    return cube.transpose(2, 0, 1, 3, 4).reshape(bricks_dev * EDGE**3, width)


def depth_pad(block):
    return jnp.pad(block, ((0, 0), (0, 0), (1, 1), (0, 0)))


def shards(features, active, weight, cotangent):
    sub_count = lax.axis_size("sub")
    group_count = lax.axis_size("bricks")
    bricks_dev = active.shape[0]
    in_width = features.shape[1]
    out_width = weight.shape[2]
    depth = bricks_dev * EDGE
    inner_rows = bricks_dev * EDGE**3
    live_rows = jnp.repeat(active.astype(jnp.float32), EDGE**3)[:, None]
    masked_features = features * live_rows.astype(jnp.bfloat16)
    masked_grads = cotangent * live_rows.astype(jnp.bfloat16)
    feature_block = to_block(masked_features, bricks_dev)
    feature_flat = feature_block.reshape(inner_rows, in_width)
    spread = jnp.zeros((EDGE + 2, EDGE + 2, depth + 2, out_width), jnp.float32)
    for first_tap in range(3):
        products = jnp.einsum(
            "xyzc,kco->xyzko",
            feature_block,
            weight[9 * first_tap : 9 * first_tap + 9],
            preferred_element_type=jnp.float32,
        )
        for inner_tap in range(9):
            mid_tap = inner_tap // 3
            last_tap = inner_tap % 3
            spread = spread.at[
                2 - first_tap : 2 - first_tap + EDGE,
                2 - mid_tap : 2 - mid_tap + EDGE,
                2 - last_tap : 2 - last_tap + depth,
            ].add(products[:, :, :, inner_tap])
    spread = spread[:, :, 1:-1]
    from_above = from_behind(spread[0].astype(jnp.bfloat16), "bricks", -1).astype(jnp.float32)
    from_below = from_behind(spread[EDGE + 1].astype(jnp.bfloat16), "bricks", 1).astype(jnp.float32)
    middle = spread[1 : EDGE + 1]
    middle = middle.at[EDGE - 1].add(from_above).at[0].add(from_below)
    from_right = from_behind(middle[:, 0].astype(jnp.bfloat16), "sub", -1).astype(jnp.float32)
    from_left = from_behind(middle[:, EDGE + 1].astype(jnp.bfloat16), "sub", 1).astype(jnp.float32)
    summed_block = middle[:, 1 : EDGE + 1].at[:, EDGE - 1].add(from_right).at[:, 0].add(from_left)
    conv_out = (to_rows(summed_block, bricks_dev) * live_rows).astype(jnp.bfloat16)
    grad_pad = depth_pad(padded(to_block(masked_grads, bricks_dev), (("bricks", 0), ("sub", 1)), 1))
    back_sum = jnp.zeros((inner_rows, in_width), jnp.float32)
    kernel_pieces = []
    for first_tap in range(3):
        columns = jnp.stack(
            [
                grad_pad[
                    2 - first_tap : 2 - first_tap + EDGE,
                    2 - mid_tap : 2 - mid_tap + EDGE,
                    2 - last_tap : 2 - last_tap + depth,
                ]
                for mid_tap in range(3)
                for last_tap in range(3)
            ],
            axis=3,
        ).reshape(inner_rows, 9, out_width)
        weight_block = weight[9 * first_tap : 9 * first_tap + 9]
        back_sum = back_sum + jnp.einsum(
            "rko,kco->rc", columns, weight_block, preferred_element_type=jnp.float32
        )
        kernel_pieces.append(
            jnp.einsum("rc,rko->kco", feature_flat, columns, preferred_element_type=jnp.float32)
        )
    kernel_local = jnp.concatenate(kernel_pieces, axis=0)
    back_rows = to_rows(back_sum.reshape(EDGE, EDGE, depth, in_width), bricks_dev)
    grad_features = (back_rows * live_rows).astype(jnp.bfloat16)
    grad_scale = 1.0 / math.sqrt(sub_count * group_count * inner_rows)
    grad_weight = (lax.psum(kernel_local, ("bricks", "sub")) * grad_scale).astype(jnp.bfloat16)
    return (conv_out, grad_features, grad_weight)


def solution(mesh):
    in_specs = (
        P(("groups", "bricks", "sub"), None),
        P(("groups", "bricks", "sub")),
        P(),
        P(("groups", "bricks", "sub"), None),
    )
    out_specs = (
        P(("groups", "bricks", "sub"), None),
        P(("groups", "bricks", "sub"), None),
        P("groups", None, None),
    )
    return jax.shard_map(shards, mesh=mesh, in_specs=in_specs, out_specs=out_specs, check_vma=False)
```

profile of v0, /device:TPU:1, one launch (start us, length us, event | category | flops | bytes accessed | tf_op | source)
XLA Modules:
  0.0 228.0 jit_solution(15235727270291543143)
XLA Ops:
  8.1 1.1 broadcast_multiply_fusion.1
  9.3 1.3 collective-permute-start.5
  10.6 4.7 %collective-permute-start.4 = (bf16[1,8,16,128]{3,2,1,0:T(8,128)(2,1)S(1)}, bf16[1,8,16,128]{3,2,1,0:T(8,128)(2,1)S(1)}, u32[]{:S(2)}, u32[]{:S(2)}) collective-permute-start(bf16[1,8,16,128]{3,2,1,0:T(8,128)(2,1)S(1)} %get-tuple-element.415), channel_id=1, source_target_pairs={{0,4},{4,8},{8,12},{1,5},{5,9},{9,13},{2,6},{6,10},{10,14},{3,7},{... | collective-permute-start | bytes 98312 | tf_op jit(solution)/shard_map/ppermute | solution.py:24
  15.3 1.2 broadcast_multiply_fusion
  17.4 3.4 %fusion.11 = f32[8,8,16,9,128]{4,2,1,0,3:T(8,128)} fusion(bf16[27,256,128]{2,1,0:T(8,128)(2,1)S(1)} %copy-done.1, bf16[8,8,2,8,256]{4,3,1,0,2:T(8,128)(2,1)S(1)} %bitcast.284), kind=kOutput, calls=%fused_computation.24 | convolution fusion | flops 603979776 | bytes 5832704 | tf_op jit(solution)/shard_map/xyzc,kco->xyzko/dot_general | solution.py:61
  20.8 3.1 %fusion.9 = f32[8,8,16,9,128]{4,2,1,0,3:T(8,128)} fusion(bf16[27,256,128]{2,1,0:T(8,128)(2,1)S(1)} %copy-done.1, bf16[8,8,2,8,256]{4,3,1,0,2:T(8,128)(2,1)S(1)} %bitcast.285), kind=kOutput, calls=%fused_computation.22 | convolution fusion | flops 603979776 | bytes 5832704 | tf_op jit(solution)/shard_map/xyzc,kco->xyzko/dot_general | solution.py:61
  24.1 1.7 scatter-add.105
  25.8 1.2 fusion.48
  27.0 1.1 fusion.46
  28.1 1.7 scatter-add.109
  29.8 1.1 fusion.45
  31.0 1.7 scatter-add.110
  32.6 1.2 fusion.44
  33.8 1.1 fusion.42
  34.9 1.7 scatter-add.114
  36.6 1.1 fusion.41
  37.8 1.7 scatter-add.115
  39.5 1.2 fusion.40
  40.6 1.1 fusion.38
  41.8 1.7 scatter-add.119
  43.5 1.1 fusion.37
  44.6 1.7 scatter-add.120
  46.3 1.1 fusion.36
  47.4 1.1 fusion.34
  48.5 1.7 scatter-add.124
  50.2 1.1 fusion.33
  51.4 1.7 scatter-add.125
  53.1 1.1 fusion.32
  54.2 1.1 fusion.30
  55.3 1.7 scatter-add.129
  57.0 1.1 fusion.29
  58.1 1.7 scatter-add.130
  59.8 1.1 fusion.28
  61.0 1.1 fusion.26
  62.1 1.7 scatter-add.134
  63.8 1.1 fusion.25
  64.9 1.7 scatter-add.135
  66.6 1.1 fusion.24
  68.4 3.1 %fusion.22 = f32[8,8,16,128]{3,2,1,0:T(8,128)S(1)} fusion(f32[8,8,16,9,128]{4,2,1,0,3:T(8,128)} %fusion.9, f32[10,10,18,128]{3,2,1,0:T(8,128)S(1)} %fusion.24, s32[]{:T(128)} %bitcast.33, s32[]{:T(128)} %bitcast.34, s32[]{:T(128)} %bitcast.35), kind=kLoop, calls=%fused_computation.41 | loop fusion | flops 131072 | bytes 1572876 | tf_op jit(solution)/shard_map/add | solution.py:74
  71.5 3.6 %scatter-add.139 = f32[10,10,18,128]{3,2,1,0:T(8,128)S(1)} dynamic-update-slice(f32[10,10,18,128]{3,2,1,0:T(8,128)S(1)} %fusion.24, f32[8,8,16,128]{3,2,1,0:T(8,128)S(1)} %fusion.22, s32[]{:T(128)} %bitcast.33, s32[]{:T(128)} %bitcast.34, s32[]{:T(128)} %bitcast.35, s32[]{:T(128)} %constant.986.clone.1) | dynamic-update-slice | bytes 1048580 | tf_op jit(solution)/shard_map/scatter-add | solution.py:74
  75.1 1.1 fusion.21
  76.2 1.7 scatter-add.140
  77.9 1.1 fusion.20
  79.1 1.1 fusion.18
  80.2 1.7 scatter-add.144
  81.9 1.1 fusion.17
  83.0 1.7 scatter-add.145
  84.7 1.1 fusion.16
  86.0 1.3 collective-permute-start
  87.3 4.0 %collective-permute-start.1 = (bf16[10,16,128]{2,1,0:T(8,128)(2,1)S(1)}, bf16[10,16,128]{2,1,0:T(8,128)(2,1)S(1)}, u32[]{:S(2)}, u32[]{:S(2)}) collective-permute-start(bf16[10,16,128]{2,1,0:T(8,128)(2,1)S(1)} %get-tuple-element.396), channel_id=1, source_target_pairs={{0,4},{4,8},{8,12},{1,5},{5,9},{9,13},{2,6},{6,10},{10,14},{3,7},{... | collective-permute-start | bytes 122888 | tf_op jit(solution)/shard_map/ppermute | solution.py:14
  91.4 3.4 %collective-permute-start.7 = (bf16[10,1,16,128]{3,2,1,0:T(8,128)(2,1)S(1)}, bf16[10,1,16,128]{3,2,1,0:T(8,128)(2,1)S(1)}, u32[]{:S(2)}, u32[]{:S(2)}) collective-permute-start(bf16[10,1,16,128]{3,2,1,0:T(8,128)(2,1)S(1)} %get-tuple-element.407), channel_id=1, source_target_pairs={{1,0},{2,1},{3,2},{5,4},{6,5},{7,6},{9,8},{10,9},{11,10},{13,12},{... | collective-permute-start | bytes 122888 | tf_op jit(solution)/shard_map/ppermute | solution.py:25
  94.9 3.6 %collective-permute-start.6 = (bf16[10,1,16,128]{3,2,1,0:T(8,128)(2,1)S(1)}, bf16[10,1,16,128]{3,2,1,0:T(8,128)(2,1)S(1)}, u32[]{:S(2)}, u32[]{:S(2)}) collective-permute-start(bf16[10,1,16,128]{3,2,1,0:T(8,128)(2,1)S(1)} %get-tuple-element.406), channel_id=1, source_target_pairs={{0,1},{1,2},{2,3},{4,5},{5,6},{6,7},{8,9},{9,10},{10,11},{12,13},{... | collective-permute-start | bytes 122888 | tf_op jit(solution)/shard_map/ppermute | solution.py:24
  99.6 1.9 collective-permute-start.2
  101.5 3.6 %collective-permute-start.3 = (bf16[8,16,128]{2,1,0:T(8,128)(2,1)S(1)}, bf16[8,16,128]{2,1,0:T(8,128)(2,1)S(1)}, u32[]{:S(2)}, u32[]{:S(2)}) collective-permute-start(bf16[8,16,128]{2,1,0:T(8,128)(2,1)S(1)} %get-tuple-element.408), channel_id=1, source_target_pairs={{0,1},{1,2},{2,3},{4,5},{5,6},{6,7},{8,9},{9,10},{10,11},{12,13},{... | collective-permute-start | bytes 98312 | tf_op jit(solution)/shard_map/ppermute | solution.py:14
  110.7 2.0 pad_maximum_fusion
  113.4 1.5 fusion.62
  114.9 1.1 copy.37
  116.0 3.2 %convolution_bitcast_fusion.3 = f32[1024,256]{1,0:T(8,128)S(1)} fusion(bf16[1024,9,128]{2,0,1:T(8,128)(2,1)} %copy-done.5, bf16[27,256,128]{2,1,0:T(8,128)(2,1)} %param.68), kind=kOutput, calls=%fused_computation.7 | convolution fusion | flops 603979776 | bytes 3997696 | tf_op jit(solution)/shard_map/rko,kco->rc/dot_general | solution.py:101
  120.4 0.9 fusion.1
  121.4 0.9 fusion.51
  122.4 1.0 fusion.3
  123.3 93.1 %all-reduce.4.cloned.1.call-done = f32[27,256,128]{1,2,0:T(8,128)} async-done(((f32[27,256,128]{1,2,0:T(8,128)}), f32[27,256,128]{1,2,0:T(8,128)}) %all-reduce.4.cloned.1.call-update) | async-done | bytes 3538960 | tf_op jit(solution)/shard_map/psum | solution.py:111
  216.5 2.4 %multiply_convert_fusion = bf16[27,256,128]{1,2,0:T(8,128)(2,1)S(1)} fusion(f32[27,256,128]{1,2,0:T(8,128)} %all-reduce.4.cloned.1.call-done), kind=kLoop, calls=%fused_computation.1 | loop fusion | flops 1769472 | bytes 5308416 | tf_op jit(solution)/shard_map/convert_element_type | solution.py:111
  218.9 2.2 copy.44
  (83 shorter events, 11.1 us)
Async XLA Ops:
  7.2 9.4 %copy-start.1 = (bf16[27,256,128]{2,1,0:T(8,128)(2,1)S(1)}, bf16[27,256,128]{2,1,0:T(8,128)(2,1)}, u32[]{:S(2)}) copy-start(bf16[27,256,128]{2,1,0:T(8,128)(2,1)} %param.68) | copy-start | bytes 5308420
  7.2 209.3 %all-reduce.4.cloned.1.call-start = ((), (), s32[]{:S(2)}) async-start(), calls=%async_computation | async-start | bytes 7077888 | tf_op jit(solution)/shard_map/psum | solution.py:111
  9.3 82.1 %collective-permute-start.5 = (bf16[1,8,16,128]{3,2,1,0:T(8,128)(2,1)S(1)}, bf16[1,8,16,128]{3,2,1,0:T(8,128)(2,1)S(1)}, u32[]{:S(2)}, u32[]{:S(2)}) collective-permute-start(bf16[1,8,16,128]{3,2,1,0:T(8,128)(2,1)S(1)} %get-tuple-element.416), channel_id=1, source_target_pairs={{4,0},{8,4},{12,8},{5,1},{9,5},{13,9},{6,2},{10,6},{14,10},{7,3},{... | collective-permute-start | bytes 98312 | tf_op jit(solution)/shard_map/ppermute | solution.py:25
  10.6 80.8 %collective-permute-start.4 = (bf16[1,8,16,128]{3,2,1,0:T(8,128)(2,1)S(1)}, bf16[1,8,16,128]{3,2,1,0:T(8,128)(2,1)S(1)}, u32[]{:S(2)}, u32[]{:S(2)}) collective-permute-start(bf16[1,8,16,128]{3,2,1,0:T(8,128)(2,1)S(1)} %get-tuple-element.415), channel_id=1, source_target_pairs={{0,4},{4,8},{8,12},{1,5},{5,9},{9,13},{2,6},{6,10},{10,14},{3,7},{... | collective-permute-start | bytes 98312 | tf_op jit(solution)/shard_map/ppermute | solution.py:24
  17.4 6.6 %copy-start = (f32[8,8,16,9,128]{4,2,3,1,0:T(8,128)}, f32[8,8,16,9,128]{4,2,3,1,0:T(8,128)S(1)}, u32[]{:S(2)}) copy-start(f32[8,8,16,9,128]{4,2,3,1,0:T(8,128)S(1)} %fusion.13) | copy-start | bytes 14155780
  86.0 12.6 %collective-permute-start = (bf16[10,16,128]{2,1,0:T(8,128)(2,1)S(1)}, bf16[10,16,128]{2,1,0:T(8,128)(2,1)S(1)}, u32[]{:S(2)}, u32[]{:S(2)}) collective-permute-start(bf16[10,16,128]{2,1,0:T(8,128)(2,1)S(1)} %get-tuple-element.397), channel_id=1, source_target_pairs={{4,0},{8,4},{12,8},{5,1},{9,5},{13,9},{6,2},{10,6},{14,10},{7,3},{... | collective-permute-start | bytes 122888 | tf_op jit(solution)/shard_map/ppermute | solution.py:14
  87.3 11.3 %collective-permute-start.1 = (bf16[10,16,128]{2,1,0:T(8,128)(2,1)S(1)}, bf16[10,16,128]{2,1,0:T(8,128)(2,1)S(1)}, u32[]{:S(2)}, u32[]{:S(2)}) collective-permute-start(bf16[10,16,128]{2,1,0:T(8,128)(2,1)S(1)} %get-tuple-element.396), channel_id=1, source_target_pairs={{0,4},{4,8},{8,12},{1,5},{5,9},{9,13},{2,6},{6,10},{10,14},{3,7},{... | collective-permute-start | bytes 122888 | tf_op jit(solution)/shard_map/ppermute | solution.py:14
  91.4 13.7 %collective-permute-start.7 = (bf16[10,1,16,128]{3,2,1,0:T(8,128)(2,1)S(1)}, bf16[10,1,16,128]{3,2,1,0:T(8,128)(2,1)S(1)}, u32[]{:S(2)}, u32[]{:S(2)}) collective-permute-start(bf16[10,1,16,128]{3,2,1,0:T(8,128)(2,1)S(1)} %get-tuple-element.407), channel_id=1, source_target_pairs={{1,0},{2,1},{3,2},{5,4},{6,5},{7,6},{9,8},{10,9},{11,10},{13,12},{... | collective-permute-start | bytes 122888 | tf_op jit(solution)/shard_map/ppermute | solution.py:25
  94.9 10.3 %collective-permute-start.6 = (bf16[10,1,16,128]{3,2,1,0:T(8,128)(2,1)S(1)}, bf16[10,1,16,128]{3,2,1,0:T(8,128)(2,1)S(1)}, u32[]{:S(2)}, u32[]{:S(2)}) collective-permute-start(bf16[10,1,16,128]{3,2,1,0:T(8,128)(2,1)S(1)} %get-tuple-element.406), channel_id=1, source_target_pairs={{0,1},{1,2},{2,3},{4,5},{5,6},{6,7},{8,9},{9,10},{10,11},{12,13},{... | collective-permute-start | bytes 122888 | tf_op jit(solution)/shard_map/ppermute | solution.py:24
  99.6 13.2 %collective-permute-start.2 = (bf16[8,16,128]{2,1,0:T(8,128)(2,1)S(1)}, bf16[8,16,128]{2,1,0:T(8,128)(2,1)S(1)}, u32[]{:S(2)}, u32[]{:S(2)}) collective-permute-start(bf16[8,16,128]{2,1,0:T(8,128)(2,1)S(1)} %get-tuple-element.409), channel_id=1, source_target_pairs={{1,0},{2,1},{3,2},{5,4},{6,5},{7,6},{9,8},{10,9},{11,10},{13,12},{... | collective-permute-start | bytes 98312 | tf_op jit(solution)/shard_map/ppermute | solution.py:14
  101.5 11.9 %collective-permute-start.3 = (bf16[8,16,128]{2,1,0:T(8,128)(2,1)S(1)}, bf16[8,16,128]{2,1,0:T(8,128)(2,1)S(1)}, u32[]{:S(2)}, u32[]{:S(2)}) collective-permute-start(bf16[8,16,128]{2,1,0:T(8,128)(2,1)S(1)} %get-tuple-element.408), channel_id=1, source_target_pairs={{0,1},{1,2},{2,3},{4,5},{5,6},{6,7},{8,9},{9,10},{10,11},{12,13},{... | collective-permute-start | bytes 98312 | tf_op jit(solution)/shard_map/ppermute | solution.py:14
  107.2 1.5 copy-start.5
  107.6 1.9 copy-start.3
  116.0 3.2 %copy-start.2 = (bf16[27,256,128]{2,1,0:T(8,128)(2,1)S(1)}, bf16[27,256,128]{2,1,0:T(8,128)(2,1)}, u32[]{:S(2)}) copy-start(bf16[27,256,128]{2,1,0:T(8,128)(2,1)} %param.68) | copy-start | bytes 5308420
  116.0 3.5 %copy-start.4 = (bf16[1024,9,128]{2,0,1:T(8,128)(2,1)S(1)}, bf16[1024,9,128]{2,0,1:T(8,128)(2,1)}, u32[]{:S(2)}) copy-start(bf16[1024,9,128]{2,0,1:T(8,128)(2,1)} %copy-done.3) | copy-start | bytes 7077892
Sparse Core Ops, SparseCore 0:
  112.9 103.5 all-reduce.3
where the time goes:
time: 232 us; the launch traced here: 228 us
  waiting for transfers between devices  93.2 us (40%)
  other arithmetic  42.6 us (18%)
  local copies, waits for them, and re-layouts  38.6 us (17%)
  starting transfers between devices  23.9 us (10%)
  between operations  15 us (6%)
  matrix products  14.8 us (6%)
    psum x1, waiting for transfers between devices, shards(): lax.psum(kernel_local, ('bricks', 'sub')) * grad_scale  93.1 us
    scatter-add x18, local copies, waits for them, and re-layouts, shards(): spread = spread.at[2 - first_tap:2 - first_tap + EDGE, 2 - mid_tap:2 - mi...  30.7 us
    add x17, other arithmetic, shards(): spread = spread.at[2 - first_tap:2 - first_tap + EDGE, 2 - mid_tap:2 - mi...  20 us
    ppermute x4, starting transfers between devices, from_behind(): return lax.ppermute(x, axis, pairs)  10.8 us
    scatter-add x9, other arithmetic, shards(): spread = spread.at[2 - first_tap:2 - first_tap + EDGE, 2 - mid_tap:2 - mi...  10.4 us
    ppermute x2, starting transfers between devices, padded(): before = lax.ppermute(last, axis, up)  8.29 us
    dot_general x3, matrix products, shards(): jnp.einsum('xyzc,kco->xyzko', feature_block, weight[9 * first_tap:9 * fir...  7.35 us
    dot_general x3, matrix products, shards(): jnp.einsum('rko,kco->rc', columns, weight_block, preferred_element_type=j...  4.94 us
  transfers between devices with their start and end apart: 9, of which 1 were waited for; matrix products, arithmetic and copies ran while one was open for 39% of the time, Pallas kernels for 0%

commit v1 on v0

v1 whole, which is shorter than its diff:
```python
import functools
import math

import jax
import jax.numpy as jnp
from jax import lax
from jax.experimental import pallas as pl
from jax.experimental.pallas import tpu as pltpu
from jax.sharding import PartitionSpec as P

EDGE = 8
MESH = pl.DeviceIdType.MESH
X_TYPE = jnp.bfloat16
Z_TYPE = jnp.float32
SIDES = [(i, j) for i in (-1, 0, 1) for j in (-1, 0, 1) if (i, j) != (0, 0)]


def own_side(step):
    return pl.ds(1, EDGE) if step == 0 else pl.ds(EDGE if step > 0 else 1, 1)


def far_side(step):
    return pl.ds(1, EDGE) if step == 0 else pl.ds(0 if step > 0 else EDGE + 1, 1)


def kernel(
    n, m, fused, grad_scale,
    feat_ref, act_ref, weight_hbm, cot_ref,
    conv_ref, gfeat_ref, gw_hbm,
    fp, gp, gcat, ft, w_ref, conv_acc, back_acc, ks, r1, s2, r2, kept, s3, r3, out,
    halo_send, halo_recv, send, recv, local_sem,
):
    g, b, s = lax.axis_index("groups"), lax.axis_index("bricks"), lax.axis_index("sub")
    bricks_dev = act_ref.shape[0]
    depth = bricks_dev * EDGE
    brick_rows = EDGE**3
    cin, cout = feat_ref.shape[1], cot_ref.shape[1]
    plane = EDGE * depth
    rows = EDGE * plane

    def inside(db, ds):
        return (b + db >= 0) & (b + db < n) & (s + ds >= 0) & (s + ds < m)

    w_copy = pltpu.make_async_copy(weight_hbm, w_ref, local_sem.at[0])
    w_copy.start()
    for field in (fp, gp):
        edge_row = jnp.zeros((EDGE + 2, depth, field.shape[3]), jnp.bfloat16)
        edge_col = jnp.zeros((EDGE, 1, depth, field.shape[3]), jnp.bfloat16)
        field[0] = edge_row
        field[EDGE + 1] = edge_row
        field[1 : EDGE + 1, 0:1] = edge_col
        field[1 : EDGE + 1, EDGE + 1 : EDGE + 2] = edge_col

    barrier = pltpu.get_barrier_semaphore()
    if fused:
        for i in range(n):
            for j in range(m):
                if (i, j) != (0, 0):
                    pl.semaphore_signal(
                        barrier, inc=1, device_id=(g, lax.rem(b + i, n), lax.rem(s + j, m)), device_id_type=MESH
                    )
    else:
        for db, ds in SIDES:
            @pl.when(inside(db, ds))
            def _():
                pl.semaphore_signal(barrier, inc=1, device_id=(g, b + db, s + ds), device_id_type=MESH)

    def place(source, target):
        def one(i, _):
            pieces = []
            for l in range(bricks_dev):
                start = pl.multiple_of(l * brick_rows + i * EDGE * EDGE, EDGE * EDGE)
                piece = source[pl.ds(start, EDGE * EDGE), :].astype(jnp.float32)
                piece = piece * act_ref[l].astype(jnp.float32)
                pieces.append(piece.reshape(EDGE, 1, EDGE, source.shape[1]))
            both = jnp.concatenate(pieces, axis=1).reshape(EDGE, depth, source.shape[1])
            target[i + 1, 1 : EDGE + 1] = both.astype(jnp.bfloat16)
            return 0

        lax.fori_loop(0, EDGE, one, 0)

    place(cot_ref, gp)
    place(feat_ref, fp)

    if fused:
        pl.semaphore_wait(barrier, n * m - 1)
    else:
        for db, ds in SIDES:
            @pl.when(inside(db, ds))
            def _():
                pl.semaphore_wait(barrier, 1)

    def halo(field_at, side):
        field = (gp, fp)[field_at]
        db, ds = SIDES[side]
        return pltpu.make_async_remote_copy(
            src_ref=field.at[own_side(db), own_side(ds)],
            dst_ref=field.at[far_side(db), far_side(ds)],
            send_sem=halo_send.at[field_at, side],
            recv_sem=halo_recv.at[field_at, side],
            device_id=(g, b + db, s + ds),
            device_id_type=MESH,
        )

    for field_at in range(2):
        for side, (db, ds) in enumerate(SIDES):
            @pl.when(inside(db, ds))
            def _():
                halo(field_at, side).start()

    def wait_halo(field_at):
        for side, (db, ds) in enumerate(SIDES):
            @pl.when(inside(-db, -ds))
            def _():
                halo(field_at, side).wait_recv()

    def turn(i, _):
        start = pl.multiple_of(i * plane, plane)
        piece = fp[i + 1, 1 : EDGE + 1].reshape(plane, cin)
        ft[:, pl.ds(start, plane)] = piece.astype(jnp.float32).T.astype(jnp.bfloat16)
        return 0

    lax.fori_loop(0, EDGE, turn, 0)
    wait_halo(0)

    def widen(i, _):
        count = (EDGE + 2) * depth
        middle = gp[i].astype(jnp.float32).reshape(count, cout)
        at = lax.rem(lax.broadcasted_iota(jnp.int32, (count, cout), 0), depth)
        later = jnp.where(at == depth - 1, 0.0, pltpu.roll(middle, count - 1, 0))
        earlier = jnp.where(at == 0, 0.0, pltpu.roll(middle, 1, 0))
        wide = jnp.concatenate([later, middle, earlier], axis=1)
        gcat[i] = wide.astype(jnp.bfloat16).reshape(EDGE + 2, depth, 3 * cout)
        return 0

    lax.fori_loop(0, EDGE + 2, widen, 0)

    def grads_at(p):
        first, mid = p // 3, p % 3
        return gcat[2 - first : 2 - first + EDGE, 2 - mid : 2 - mid + EDGE].reshape(rows, 3 * cout)

    def weights_at(p):
        return jnp.concatenate([w_ref[3 * p], w_ref[3 * p + 1], w_ref[3 * p + 2]], axis=1)

    def tap_sums(p):
        sums = jnp.dot(ft[...], grads_at(p), preferred_element_type=jnp.float32)
        for last in range(3):
            ks[p, last * cin : (last + 1) * cin] = sums[:, last * cout : (last + 1) * cout]

    def forward(p):
        first, mid = p // 3, p % 3
        field = fp[first : first + EDGE, mid : mid + EDGE].reshape(rows, cin)
        term = jnp.dot(field, weights_at(p), preferred_element_type=jnp.float32)
        if p == 0:
            conv_acc[...] = term
        else:
            conv_acc[...] += term

    def backward(p):
        term = lax.dot_general(
            grads_at(p), weights_at(p), (((1,), (1,)), ((), ())), preferred_element_type=jnp.float32
        )
        if p == 0:
            back_acc[...] = term
        else:
            back_acc[...] += term

    def write_rows(i, value, target):
        width = target.shape[1]
        parts = value.reshape(EDGE, bricks_dev, EDGE, width)
        for l in range(bricks_dev):
            start = pl.multiple_of(l * brick_rows + i * EDGE * EDGE, EDGE * EDGE)
            piece = parts[:, l].reshape(EDGE * EDGE, width) * act_ref[l].astype(jnp.float32)
            target[pl.ds(start, EDGE * EDGE), :] = piece.astype(jnp.bfloat16)

    def write_forward():
        def one(i, _):
            start = pl.multiple_of(i * plane, plane)
            at = lax.rem(lax.broadcasted_iota(jnp.int32, (plane, cout), 0), depth)
            before = conv_acc[pl.ds(start, plane), 0:cout]
            middle = conv_acc[pl.ds(start, plane), cout : 2 * cout]
            after = conv_acc[pl.ds(start, plane), 2 * cout : 3 * cout]
            value = middle + jnp.where(at == 0, 0.0, pltpu.roll(before, 1, 0))
            value = value + jnp.where(at == depth - 1, 0.0, pltpu.roll(after, plane - 1, 0))
            write_rows(i, value, conv_ref)
            return 0

        lax.fori_loop(0, EDGE, one, 0)

    def write_backward():
        def one(i, _):
            start = pl.multiple_of(i * plane, plane)
            write_rows(i, back_acc[pl.ds(start, plane), :], gfeat_ref)
            return 0

        lax.fori_loop(0, EDGE, one, 0)

    jobs = [functools.partial(backward, p) for p in range(9)] + [write_backward]
    jobs += [functools.partial(forward, p) for p in range(9)] + [write_forward]
    jobs[0:0] = [w_copy.wait]
    jobs[11:11] = [lambda: wait_halo(1)]

    if not fused:
        for p in range(9):
            tap_sums(p)
        for job in jobs:
            job()
        local = pltpu.make_async_copy(ks, gw_hbm, local_sem.at[1])
        local.start()
        local.wait()
    else:
        core = lax.rem(s, 2)
        x = s // 2
        group_rows = 3 * cin
        half, quarter = group_rows // 2, group_rows // 4
        chunk = quarter // n
        twin = (g, b, s + 1 - 2 * core)
        across = (g, b, lax.rem(s + 2, m))

        def aligned(value):
            return pl.multiple_of(value, 16)

        def along(step):
            return (g, lax.rem(b + step, n), s)

        def remote(p, slot, src, dst, device):
            return pltpu.make_async_remote_copy(
                src_ref=src, dst_ref=dst, send_sem=send.at[p, slot], recv_sem=recv.at[p, slot],
                device_id=device, device_id_type=MESH,
            )

        mine = aligned(core * half)
        mine_x = aligned(core * half + x * quarter)
        mine_z = aligned(core * half + x * quarter + b * chunk)

        def pair_copy(p):
            return remote(p, 0, ks.at[p, pl.ds(aligned((1 - core) * half), half)], r1.at[p], twin)

        def across_copy(p):
            return remote(p, 1, s2.at[p], r2.at[p], across)

        def along_copy(p, step):
            to = lax.rem(b + step, n)
            return remote(p, 1 + step, s3.at[p, to], r3.at[p, step - 1], along(step))

        def along_back(p, step):
            part = out.at[p, pl.ds(mine_z, chunk)]
            return remote(p, n + step, part, part, along(step))

        def across_back(p):
            part = out.at[p, pl.ds(mine_x, quarter)]
            return remote(p, 2 * n, part, part, across)

        def pair_back(p):
            part = out.at[p, pl.ds(mine, half)]
            return remote(p, 2 * n + 1, part, part, twin)

        def write_out(p):
            return pltpu.make_async_copy(out.at[p], gw_hbm.at[p], local_sem.at[1 + p])

        def stage0(p):
            tap_sums(p)
            pair_copy(p).start()

        def stage1(p):
            pair_copy(p).wait_recv()
            theirs = aligned((1 - x) * quarter)
            total = ks[p, pl.ds(aligned(core * half + (1 - x) * quarter), quarter)] + r1[p, pl.ds(theirs, quarter)]
            s2[p] = total.astype(X_TYPE)
            across_copy(p).start()
            kept[p] = ks[p, pl.ds(mine_x, quarter)] + r1[p, pl.ds(aligned(x * quarter), quarter)]

        def stage2(p):
            across_copy(p).wait_recv()
            total = kept[p] + r2[p].astype(jnp.float32)
            kept[p] = total
            s3[p] = total.astype(Z_TYPE).reshape(n, chunk, cout)
            for step in range(1, n):
                along_copy(p, step).start()

        def stage3(p):
            total = kept[p, pl.ds(aligned(b * chunk), chunk)]
            for step in range(1, n):
                along_copy(p, step).wait_recv()
                total = total + r3[p, step - 1].astype(jnp.float32)
            out[p, pl.ds(mine_z, chunk)] = (total * grad_scale).astype(jnp.bfloat16)
            for step in range(1, n):
                along_back(p, step).start()

        def stage4(p):
            for step in range(1, n):
                along_back(p, step).wait_recv()
            across_back(p).start()

        def stage5(p):
            across_back(p).wait_recv()
            pair_back(p).start()

        def stage6(p):
            pair_back(p).wait_recv()
            write_out(p).start()

        stages = [stage0, stage1, stage2, stage3, stage4, stage5, stage6]
        for t in range(9 + 6):
            for k in reversed(range(7)):
                if 0 <= t - k < 9:
                    stages[k](t - k)
            if t >= 1:
                for job in jobs[:2]:
                    job()
                jobs = jobs[2:]
        for job in jobs:
            job()
        for p in range(9):
            pair_copy(p).wait_send()
            across_copy(p).wait_send()
            for step in range(1, n):
                along_copy(p, step).wait_send()
                along_back(p, step).wait_send()
            across_back(p).wait_send()
            pair_back(p).wait_send()
            write_out(p).wait()

    for field_at in range(2):
        for side, (db, ds) in enumerate(SIDES):
            @pl.when(inside(db, ds))
            def _():
                halo(field_at, side).wait_send()


def shards(features, active, weight, cotangent):
    n, m = lax.axis_size("bricks"), lax.axis_size("sub")
    bricks_dev = active.shape[0]
    cin, cout = features.shape[1], weight.shape[2]
    rows = features.shape[0]
    depth = bricks_dev * EDGE
    group_rows = 3 * cin
    fused = m == 4 and group_rows % (4 * n * 16) == 0
    quarter = group_rows // 4
    chunk = quarter // n if fused else 16
    slots = 2 * n + 2 if fused else 1
    groups = 9 if fused else 1
    grad_scale = 1.0 / math.sqrt(n * m * rows)
    bf16, f32 = jnp.bfloat16, jnp.float32
    vmem = pl.BlockSpec(memory_space=pltpu.VMEM)
    scratch = [
        pltpu.VMEM((EDGE + 2, EDGE + 2, depth, cin), bf16),
        pltpu.VMEM((EDGE + 2, EDGE + 2, depth, cout), bf16),
        pltpu.VMEM((EDGE + 2, EDGE + 2, depth, 3 * cout), bf16),
        pltpu.VMEM((cin, rows), bf16),
        pltpu.VMEM(weight.shape, bf16),
        pltpu.VMEM((rows, 3 * cout), f32),
        pltpu.VMEM((rows, cin), f32),
        pltpu.VMEM((9, group_rows, cout), f32),
        pltpu.VMEM((groups, group_rows // 2, cout), f32),
        pltpu.VMEM((groups, quarter, cout), X_TYPE),
        pltpu.VMEM((groups, quarter, cout), X_TYPE),
        pltpu.VMEM((groups, quarter, cout), f32),
        pltpu.VMEM((groups, n, chunk, cout), Z_TYPE),
        pltpu.VMEM((groups, n - 1, chunk, cout), Z_TYPE),
        pltpu.VMEM((groups, group_rows, cout), bf16),
        pltpu.SemaphoreType.DMA((2, 8)),
        pltpu.SemaphoreType.DMA((2, 8)),
        pltpu.SemaphoreType.DMA((groups, slots)),
        pltpu.SemaphoreType.DMA((groups, slots)),
        pltpu.SemaphoreType.DMA((10,)),
    ]
    conv_out, grad_features, grad_weight = pl.pallas_call(
        functools.partial(kernel, n, m, fused, grad_scale),
        out_shape=(
            jax.ShapeDtypeStruct((rows, cout), bf16),
            jax.ShapeDtypeStruct((rows, cin), bf16),
            jax.ShapeDtypeStruct((9, group_rows, cout), bf16 if fused else f32),
        ),
        in_specs=[vmem, pl.BlockSpec(memory_space=pltpu.SMEM), pl.BlockSpec(memory_space=pl.ANY), vmem],
        out_specs=(vmem, vmem, pl.BlockSpec(memory_space=pl.ANY)),
        scratch_shapes=scratch,
        compiler_params=pltpu.CompilerParams(
            collective_id=0, has_side_effects=True, vmem_limit_bytes=48 * 1024 * 1024
        ),
    )(features, active, weight, cotangent)
    grad_weight = grad_weight.reshape(27, cin, cout)
    if not fused:
        grad_weight = (lax.psum(grad_weight, ("bricks", "sub")) * grad_scale).astype(bf16)
    return (conv_out, grad_features, grad_weight)


def solution(mesh):
    in_specs = (
        P(("groups", "bricks", "sub"), None),
        P(("groups", "bricks", "sub")),
        P(),
        P(("groups", "bricks", "sub"), None),
    )
    out_specs = (
        P(("groups", "bricks", "sub"), None),
        P(("groups", "bricks", "sub"), None),
        P("groups", None, None),
    )
    return jax.shard_map(shards, mesh=mesh, in_specs=in_specs, out_specs=out_specs, check_vma=False)
```

time: 232 us -> 74.8 us (0.32); the launches traced: 228 us -> 74.6 us
  waiting for transfers between devices: 93.2 us -> 0 us
  Pallas kernels: 0 us -> 67.1 us
  other arithmetic: 42.6 us -> 0 us
  local copies, waits for them, and re-layouts: 38.6 us -> 6.82 us
  starting transfers between devices: 23.9 us -> 0 us
  matrix products: 14.8 us -> 0 us
  between operations: 15 us -> 0.65 us
    psum x1 -> x0, waiting for transfers between devices: 93.1 us -> none  [shards(): lax.psum(kernel_local, ('bricks', 'sub')) * grad_scale]
    pallas_call x0 -> x1, Pallas kernels: none -> 67.1 us  [shards(): pl.pallas_call(functools.partial(kernel, n, m, fused, grad_scale), out_sh...]
    scatter-add x18 -> x0, local copies, waits for them, and re-layouts: 30.7 us -> none  [shards(): spread = spread.at[2 - first_tap:2 - first_tap + EDGE, 2 - mid_tap:2 - mi...]
    ppermute x8 -> x0, starting transfers between devices: 23.9 us -> none  [the longest x4 10.8 us: from_behind(): return lax.ppermute(x, axis, pairs)]
    add x17 -> x0, other arithmetic: 20 us -> none  [shards(): spread = spread.at[2 - first_tap:2 - first_tap + EDGE, 2 - mid_tap:2 - mi...]
    dot_general x9 -> x0, matrix products: 14.8 us -> none  [the longest x3 7.35 us: shards(): jnp.einsum('xyzc,kco->xyzko', feature_block, weight[9 * first_tap:9 * fir...]
    scatter-add x13 -> x0, other arithmetic: 12.5 us -> none  [the longest x9 10.4 us: shards(): spread = spread.at[2 - first_tap:2 - first_tap + EDGE, 2 - mid_tap:2 - mi...]
    convert_element_type x5 -> x0, other arithmetic: 5.13 us -> none  [the longest x1 2.44 us: shards(): (lax.psum(kernel_local, ('bricks', 'sub')) * grad_scale).astype(jnp.bfloa...]
  transfers between devices with their start and end apart: 9 -> 0, of which waited for: 1 -> 0; matrix products, arithmetic and copies ran while one was open for 39% -> 0% of each run, Pallas kernels for 0% -> 0%
where the time goes in v1:
time: 74.8 us; the launch traced here: 74.6 us
  Pallas kernels  67.1 us (90%)
  local copies, waits for them, and re-layouts  6.82 us (9%)
    pallas_call x1, Pallas kernels, shards(): pl.pallas_call(functools.partial(kernel, n, m, fused, grad_scale), out_sh...  67.1 us
    unnamed x11, local copies, waits for them, and re-layouts  6.82 us

profile of v1, /device:TPU:1, one launch (start us, length us, event | category | flops | bytes accessed | tf_op | source)
XLA Modules:
  0.0 74.6 jit_solution(1213517446248985681)
XLA Ops:
  0.6 0.0 copy-start
  0.6 1.5 %copy-done = bf16[27,256,128]{2,1,0:T(8,128)(2,1)S(1)} copy-done((bf16[27,256,128]{2,1,0:T(8,128)(2,1)S(1)}, bf16[27,256,128]{2,1,0:T(8,128)(2,1)}, u32[]{:S(2)}) %copy-start) | copy-done | bytes 1769496
  2.1 0.0 copy-start.1
  2.1 1.0 %copy-done.1 = bf16[1024,256]{1,0:T(8,128)(2,1)S(1)} copy-done((bf16[1024,256]{1,0:T(8,128)(2,1)S(1)}, bf16[1024,256]{1,0:T(8,128)(2,1)}, u32[]{:S(2)}) %copy-start.1) | copy-done | bytes 524312
  3.2 0.0 copy-start.2
  3.2 0.9 %copy-done.2 = bf16[1024,128]{1,0:T(8,128)(2,1)S(1)} copy-done((bf16[1024,128]{1,0:T(8,128)(2,1)S(1)}, bf16[1024,128]{1,0:T(8,128)(2,1)}, u32[]{:S(2)}) %copy-start.2) | copy-done | bytes 262168
  4.1 0.0 copy-start.3
  4.1 0.7 copy-done.3
  4.8 67.1 %shard_map.67 = (bf16[1024,128]{1,0:T(8,128)(2,1)S(1)}, bf16[1024,256]{1,0:T(8,128)(2,1)S(1)}, bf16[9,768,128]{2,1,0:T(8,128)(2,1)S(1)}) custom-call(bf16[1024,256]{1,0:T(8,128)(2,1)S(1)} %copy-done.1, s32[2]{0:T(128)S(1)} %copy-done.3, bf16[27,256,128]{2,1,0:T(8,128)(2,1)S(1)} %copy-done, bf16[1024,128]{1,0:T(8,128)(2,1)S(1)} %copy-done.2), custom_call_target="tpu_custom_call" | custom-call | tf_op jit(solution)/shard_map/pallas_call | solution.py:368
  71.9 0.7 copy.10
  72.6 0.8 %copy.11 = bf16[1024,256]{1,0:T(8,128)(2,1)} copy(bf16[1024,256]{1,0:T(8,128)(2,1)S(1)} %get-tuple-element.13) | data formatting | bytes 1048576
  73.4 1.2 %copy.12 = bf16[27,256,128]{2,1,0:T(8,128)(2,1)} copy(bf16[27,256,128]{2,1,0:T(8,128)(2,1)S(1)} %bitcast.1) | data formatting | bytes 3538944
Async XLA Ops:
  0.6 1.5 %copy-start = (bf16[27,256,128]{2,1,0:T(8,128)(2,1)S(1)}, bf16[27,256,128]{2,1,0:T(8,128)(2,1)}, u32[]{:S(2)}) copy-start(bf16[27,256,128]{2,1,0:T(8,128)(2,1)} %weight_hbm.1) | copy-start | bytes 5308420
  2.1 1.0 %copy-start.1 = (bf16[1024,256]{1,0:T(8,128)(2,1)S(1)}, bf16[1024,256]{1,0:T(8,128)(2,1)}, u32[]{:S(2)}) copy-start(bf16[1024,256]{1,0:T(8,128)(2,1)} %feat_ref.1) | copy-start | bytes 1572868
  3.2 0.9 %copy-start.2 = (bf16[1024,128]{1,0:T(8,128)(2,1)S(1)}, bf16[1024,128]{1,0:T(8,128)(2,1)}, u32[]{:S(2)}) copy-start(bf16[1024,128]{1,0:T(8,128)(2,1)} %cot_ref.1) | copy-start | bytes 786436
  4.1 0.7 copy-start.3

commit v2 on v1

--- a/solution.py
+++ b/solution.py
@@ -10,8 +10,11 @@
 
 EDGE = 8
 MESH = pl.DeviceIdType.MESH
-X_TYPE = jnp.bfloat16
-Z_TYPE = jnp.float32
+LEVELS = 4
+WIRE = (jnp.float32, jnp.bfloat16, jnp.float32, jnp.float32)
+STARTS = (0, 2, 4, 6, 8, 10, 12, 14, 16)
+PER_STEP = 1
+VMEM_LIMIT = 60 * 1024 * 1024
 SIDES = [(i, j) for i in (-1, 0, 1) for j in (-1, 0, 1) if (i, j) != (0, 0)]
 
 
@@ -25,10 +28,10 @@
 
 def kernel(
     n, m, fused, grad_scale,
-    feat_ref, act_ref, weight_hbm, cot_ref,
+    feat_hbm, act_ref, weight_hbm, cot_hbm,
     conv_ref, gfeat_ref, gw_hbm,
-    fp, gp, gcat, ft, w_ref, conv_acc, back_acc, ks, r1, s2, r2, kept, s3, r3, out,
-    halo_send, halo_recv, send, recv, local_sem,
+    feat_ref, cot_ref, fp, gp, gcat, ft, w_ref, conv_acc, back_acc, ks, out,
+    got, sent, kept, halo_send, halo_recv, send, recv, local_sem,
 ):
     g, b, s = lax.axis_index("groups"), lax.axis_index("bricks"), lax.axis_index("sub")
     bricks_dev = act_ref.shape[0]
@@ -42,6 +45,10 @@
         return (b + db >= 0) & (b + db < n) & (s + ds >= 0) & (s + ds < m)
 
     w_copy = pltpu.make_async_copy(weight_hbm, w_ref, local_sem.at[0])
+    feat_copy = pltpu.make_async_copy(feat_hbm, feat_ref, local_sem.at[10])
+    cot_copy = pltpu.make_async_copy(cot_hbm, cot_ref, local_sem.at[11])
+    cot_copy.start()
+    feat_copy.start()
     w_copy.start()
     for field in (fp, gp):
         edge_row = jnp.zeros((EDGE + 2, depth, field.shape[3]), jnp.bfloat16)
@@ -79,8 +86,8 @@
 
         lax.fori_loop(0, EDGE, one, 0)
 
+    cot_copy.wait()
     place(cot_ref, gp)
-    place(feat_ref, fp)
 
     if fused:
         pl.semaphore_wait(barrier, n * m - 1)
@@ -102,11 +109,16 @@
             device_id_type=MESH,
         )
 
-    for field_at in range(2):
+    def start_halo(field_at):
         for side, (db, ds) in enumerate(SIDES):
             @pl.when(inside(db, ds))
             def _():
                 halo(field_at, side).start()
+
+    start_halo(0)
+    feat_copy.wait()
+    place(feat_ref, fp)
+    start_halo(1)
 
     def wait_halo(field_at):
         for side, (db, ds) in enumerate(SIDES):
@@ -126,7 +138,7 @@
     def widen(i, _):
         count = (EDGE + 2) * depth
         middle = gp[i].astype(jnp.float32).reshape(count, cout)
-        at = lax.rem(lax.broadcasted_iota(jnp.int32, (count, cout), 0), depth)
+        at = lax.broadcasted_iota(jnp.int32, (EDGE + 2, depth, cout), 1).reshape(count, cout)
         later = jnp.where(at == depth - 1, 0.0, pltpu.roll(middle, count - 1, 0))
         earlier = jnp.where(at == 0, 0.0, pltpu.roll(middle, 1, 0))
         wide = jnp.concatenate([later, middle, earlier], axis=1)
@@ -176,7 +188,7 @@
     def write_forward():
         def one(i, _):
             start = pl.multiple_of(i * plane, plane)
-            at = lax.rem(lax.broadcasted_iota(jnp.int32, (plane, cout), 0), depth)
+            at = lax.broadcasted_iota(jnp.int32, (EDGE, depth, cout), 1).reshape(plane, cout)
             before = conv_acc[pl.ds(start, plane), 0:cout]
             middle = conv_acc[pl.ds(start, plane), cout : 2 * cout]
             after = conv_acc[pl.ds(start, plane), 2 * cout : 3 * cout]
@@ -209,116 +221,88 @@
         local.start()
         local.wait()
     else:
-        core = lax.rem(s, 2)
-        x = s // 2
-        group_rows = 3 * cin
-        half, quarter = group_rows // 2, group_rows // 4
-        chunk = quarter // n
-        twin = (g, b, s + 1 - 2 * core)
-        across = (g, b, lax.rem(s + 2, m))
+        core, x = lax.rem(s, 2), s // 2
+        low, high = lax.rem(b, 2), b // 2
+        bits = (core, x, low, high)
+        partners = (
+            (g, b, s + 1 - 2 * core),
+            (g, b, lax.rem(s + 2, m)),
+            (g, b + 1 - 2 * low, s),
+            (g, lax.rem(b + 2, n), s),
+        )
+        sizes = [3 * cin >> (level + 1) for level in range(LEVELS)]
 
         def aligned(value):
             return pl.multiple_of(value, 16)
 
-        def along(step):
-            return (g, lax.rem(b + step, n), s)
-
-        def remote(p, slot, src, dst, device):
+        bases = [0]
+        for level in range(LEVELS):
+            bases.append(bases[level] + bits[level] * sizes[level])
+
+        def reduce_copy(p, level):
+            if level == 0:
+                src = ks.at[p, pl.ds(aligned((1 - core) * sizes[0]), sizes[0])]
+            else:
+                src = sent[level - 1].at[p]
             return pltpu.make_async_remote_copy(
-                src_ref=src, dst_ref=dst, send_sem=send.at[p, slot], recv_sem=recv.at[p, slot],
-                device_id=device, device_id_type=MESH,
+                src_ref=src, dst_ref=got[level].at[p], send_sem=send.at[p, level], recv_sem=recv.at[p, level],
+                device_id=partners[level], device_id_type=MESH,
             )
 
-        mine = aligned(core * half)
-        mine_x = aligned(core * half + x * quarter)
-        mine_z = aligned(core * half + x * quarter + b * chunk)
-
-        def pair_copy(p):
-            return remote(p, 0, ks.at[p, pl.ds(aligned((1 - core) * half), half)], r1.at[p], twin)
-
-        def across_copy(p):
-            return remote(p, 1, s2.at[p], r2.at[p], across)
-
-        def along_copy(p, step):
-            to = lax.rem(b + step, n)
-            return remote(p, 1 + step, s3.at[p, to], r3.at[p, step - 1], along(step))
-
-        def along_back(p, step):
-            part = out.at[p, pl.ds(mine_z, chunk)]
-            return remote(p, n + step, part, part, along(step))
-
-        def across_back(p):
-            part = out.at[p, pl.ds(mine_x, quarter)]
-            return remote(p, 2 * n, part, part, across)
-
-        def pair_back(p):
-            part = out.at[p, pl.ds(mine, half)]
-            return remote(p, 2 * n + 1, part, part, twin)
+        def gather_copy(p, level):
+            part = out.at[p, pl.ds(aligned(bases[level + 1]), sizes[level])]
+            return pltpu.make_async_remote_copy(
+                src_ref=part, dst_ref=part, send_sem=send.at[p, LEVELS + level],
+                recv_sem=recv.at[p, LEVELS + level], device_id=partners[level], device_id_type=MESH,
+            )
 
         def write_out(p):
             return pltpu.make_async_copy(out.at[p], gw_hbm.at[p], local_sem.at[1 + p])
 
-        def stage0(p):
-            tap_sums(p)
-            pair_copy(p).start()
-
-        def stage1(p):
-            pair_copy(p).wait_recv()
-            theirs = aligned((1 - x) * quarter)
-            total = ks[p, pl.ds(aligned(core * half + (1 - x) * quarter), quarter)] + r1[p, pl.ds(theirs, quarter)]
-            s2[p] = total.astype(X_TYPE)
-            across_copy(p).start()
-            kept[p] = ks[p, pl.ds(mine_x, quarter)] + r1[p, pl.ds(aligned(x * quarter), quarter)]
-
-        def stage2(p):
-            across_copy(p).wait_recv()
-            total = kept[p] + r2[p].astype(jnp.float32)
-            kept[p] = total
-            s3[p] = total.astype(Z_TYPE).reshape(n, chunk, cout)
-            for step in range(1, n):
-                along_copy(p, step).start()
-
-        def stage3(p):
-            total = kept[p, pl.ds(aligned(b * chunk), chunk)]
-            for step in range(1, n):
-                along_copy(p, step).wait_recv()
-                total = total + r3[p, step - 1].astype(jnp.float32)
-            out[p, pl.ds(mine_z, chunk)] = (total * grad_scale).astype(jnp.bfloat16)
-            for step in range(1, n):
-                along_back(p, step).start()
-
-        def stage4(p):
-            for step in range(1, n):
-                along_back(p, step).wait_recv()
-            across_back(p).start()
-
-        def stage5(p):
-            across_back(p).wait_recv()
-            pair_back(p).start()
-
-        def stage6(p):
-            pair_back(p).wait_recv()
-            write_out(p).start()
-
-        stages = [stage0, stage1, stage2, stage3, stage4, stage5, stage6]
-        for t in range(9 + 6):
-            for k in reversed(range(7)):
-                if 0 <= t - k < 9:
-                    stages[k](t - k)
+        def mine(p, level, start, size):
+            there = pl.ds(aligned(start), size)
+            if level == 0:
+                held = ks[p, pl.ds(aligned(core * sizes[0] + start), size)]
+            else:
+                held = kept[level - 1][p, there]
+            return held + got[level][p, there].astype(jnp.float32)
+
+        def stage(k, p):
+            if k == 0:
+                tap_sums(p)
+                reduce_copy(p, 0).start()
+            elif k < LEVELS:
+                reduce_copy(p, k - 1).wait_recv()
+                size = sizes[k]
+                sent[k - 1][p] = mine(p, k - 1, (1 - bits[k]) * size, size).astype(WIRE[k])
+                reduce_copy(p, k).start()
+                kept[k - 1][p] = mine(p, k - 1, bits[k] * size, size)
+            elif k == LEVELS:
+                reduce_copy(p, k - 1).wait_recv()
+                total = mine(p, k - 1, 0, sizes[k - 1])
+                out[p, pl.ds(aligned(bases[LEVELS]), sizes[k - 1])] = (total * grad_scale).astype(jnp.bfloat16)
+                gather_copy(p, LEVELS - 1).start()
+            elif k < 2 * LEVELS:
+                gather_copy(p, 2 * LEVELS - k).wait_recv()
+                gather_copy(p, 2 * LEVELS - k - 1).start()
+            else:
+                gather_copy(p, 0).wait_recv()
+                write_out(p).start()
+
+        for t in range(9 + STARTS[-1]):
+            for k in reversed(range(2 * LEVELS + 1)):
+                if 0 <= t - STARTS[k] < 9:
+                    stage(k, t - STARTS[k])
             if t >= 1:
-                for job in jobs[:2]:
+                for job in jobs[:PER_STEP]:
                     job()
-                jobs = jobs[2:]
+                jobs = jobs[PER_STEP:]
         for job in jobs:
             job()
         for p in range(9):
-            pair_copy(p).wait_send()
-            across_copy(p).wait_send()
-            for step in range(1, n):
-                along_copy(p, step).wait_send()
-                along_back(p, step).wait_send()
-            across_back(p).wait_send()
-            pair_back(p).wait_send()
+            for level in range(LEVELS):
+                reduce_copy(p, level).wait_send()
+                gather_copy(p, level).wait_send()
             write_out(p).wait()
 
     for field_at in range(2):
@@ -335,15 +319,17 @@
     rows = features.shape[0]
     depth = bricks_dev * EDGE
     group_rows = 3 * cin
-    fused = m == 4 and group_rows % (4 * n * 16) == 0
-    quarter = group_rows // 4
-    chunk = quarter // n if fused else 16
-    slots = 2 * n + 2 if fused else 1
+    fused = n == 4 and m == 4 and group_rows % 256 == 0
+    sizes = [group_rows >> (level + 1) for level in range(LEVELS)] if fused else [16] * LEVELS
+    slots = 2 * LEVELS
     groups = 9 if fused else 1
     grad_scale = 1.0 / math.sqrt(n * m * rows)
     bf16, f32 = jnp.bfloat16, jnp.float32
     vmem = pl.BlockSpec(memory_space=pltpu.VMEM)
+    hbm = pl.BlockSpec(memory_space=pltpu.HBM)
     scratch = [
+        pltpu.VMEM((rows, cin), bf16),
+        pltpu.VMEM((rows, cout), bf16),
         pltpu.VMEM((EDGE + 2, EDGE + 2, depth, cin), bf16),
         pltpu.VMEM((EDGE + 2, EDGE + 2, depth, cout), bf16),
         pltpu.VMEM((EDGE + 2, EDGE + 2, depth, 3 * cout), bf16),
@@ -352,18 +338,15 @@
         pltpu.VMEM((rows, 3 * cout), f32),
         pltpu.VMEM((rows, cin), f32),
         pltpu.VMEM((9, group_rows, cout), f32),
-        pltpu.VMEM((groups, group_rows // 2, cout), f32),
-        pltpu.VMEM((groups, quarter, cout), X_TYPE),
-        pltpu.VMEM((groups, quarter, cout), X_TYPE),
-        pltpu.VMEM((groups, quarter, cout), f32),
-        pltpu.VMEM((groups, n, chunk, cout), Z_TYPE),
-        pltpu.VMEM((groups, n - 1, chunk, cout), Z_TYPE),
         pltpu.VMEM((groups, group_rows, cout), bf16),
+        [pltpu.VMEM((groups, size, cout), kind) for size, kind in zip(sizes, WIRE)],
+        [pltpu.VMEM((groups, size, cout), kind) for size, kind in zip(sizes[1:], WIRE[1:])],
+        [pltpu.VMEM((groups, size, cout), f32) for size in sizes[1:]],
         pltpu.SemaphoreType.DMA((2, 8)),
         pltpu.SemaphoreType.DMA((2, 8)),
         pltpu.SemaphoreType.DMA((groups, slots)),
         pltpu.SemaphoreType.DMA((groups, slots)),
-        pltpu.SemaphoreType.DMA((10,)),
+        pltpu.SemaphoreType.DMA((12,)),
     ]
     conv_out, grad_features, grad_weight = pl.pallas_call(
         functools.partial(kernel, n, m, fused, grad_scale),
@@ -372,11 +355,11 @@
             jax.ShapeDtypeStruct((rows, cin), bf16),
             jax.ShapeDtypeStruct((9, group_rows, cout), bf16 if fused else f32),
         ),
-        in_specs=[vmem, pl.BlockSpec(memory_space=pltpu.SMEM), pl.BlockSpec(memory_space=pl.ANY), vmem],
+        in_specs=[hbm, pl.BlockSpec(memory_space=pltpu.SMEM), hbm, hbm],
         out_specs=(vmem, vmem, pl.BlockSpec(memory_space=pl.ANY)),
         scratch_shapes=scratch,
         compiler_params=pltpu.CompilerParams(
-            collective_id=0, has_side_effects=True, vmem_limit_bytes=48 * 1024 * 1024
+            collective_id=0, has_side_effects=True, vmem_limit_bytes=VMEM_LIMIT
         ),
     )(features, active, weight, cotangent)
     grad_weight = grad_weight.reshape(27, cin, cout)

time: 74.8 us -> 59.2 us (0.79)
  Pallas kernels: 67.1 us -> 51.9 us
    pallas_call x1, Pallas kernels: 67.1 us -> 51.9 us  [shards(): pl.pallas_call(functools.partial(kernel, n, m, fused, grad_scale), out_sh...]
    unnamed x11 -> x3, local copies, waits for them, and re-layouts: 6.82 us -> 6.41 us
where the time goes in v2:
time: 59.2 us; the launch traced here: 58.9 us
  Pallas kernels  51.9 us (88%)
  local copies, waits for them, and re-layouts  6.41 us (11%)
  between operations  0.64 us (1%)
    pallas_call x1, Pallas kernels, shards(): pl.pallas_call(functools.partial(kernel, n, m, fused, grad_scale), out_sh...  51.9 us
    unnamed x3, local copies, waits for them, and re-layouts  6.41 us

profile of v2, /device:TPU:1, one launch (start us, length us, event | category | flops | bytes accessed | tf_op | source)
XLA Modules:
  0.0 58.9 jit_solution(16699629845062967313)
XLA Ops:
  0.6 51.9 %shard_map.67 = (bf16[1024,128]{1,0:T(8,128)(2,1)}, bf16[1024,256]{1,0:T(8,128)(2,1)}, bf16[9,768,128]{2,1,0:T(8,128)(2,1)}) custom-call(bf16[1024,256]{1,0:T(8,128)(2,1)} %feat_hbm.1, s32[2]{0:T(128)} %act_ref.1, bf16[27,256,128]{2,1,0:T(8,128)(2,1)} %weight_hbm.1, bf16[1024,128]{1,0:T(8,128)(2,1)} %cot_hbm.1), custom_call_target="tpu_custom_call" | custom-call | tf_op jit(solution)/shard_map/pallas_call | solution.py:351
  52.5 1.7 %copy.10 = bf16[1024,128]{1,0:T(8,128)(2,1)} copy(bf16[1024,128]{1,0:T(8,128)(2,1)} %get-tuple-element.12) | data formatting | bytes 524288
  54.2 1.9 %copy.11 = bf16[1024,256]{1,0:T(8,128)(2,1)} copy(bf16[1024,256]{1,0:T(8,128)(2,1)} %get-tuple-element.13) | data formatting | bytes 1048576
  56.1 2.9 %copy.12 = bf16[27,256,128]{2,1,0:T(8,128)(2,1)} copy(bf16[27,256,128]{2,1,0:T(8,128)(2,1)} %bitcast.1) | data formatting | bytes 3538944
